TPU v7x, 256 devices: a whole 4x4x8 slice. The times are simulated.
256 devices in a mesh: gx: 8 (over x, z_hi), gy: 8 (over z_lo, core), gz: 4 (over y).
Axes of the slice: x: 4, y: 4, z: 8 (z_hi: 2, z_lo: 4; z = z_hi * 4 + z_lo), core: 2. Of those that a mesh axis runs over, the one named last changes fastest.
Arguments:
- cell_index: int32 [3, 8, 8, 4, 1024], P(None, 'gx', 'gy', 'gz'), may hold values from 0 to 127, as said below
- cell_offset: float32 [3, 8, 8, 4, 1024], P(None, 'gx', 'gy', 'gz'), may hold values from 0 to 1
- radius: float32 [8, 8, 4, 1024], P('gx', 'gy', 'gz'), may hold values from 0.3 to 0.7
- forcing: float32 [3, 8, 8, 4, 1024], P(None, 'gx', 'gy', 'gz'), may hold values from -6 to 6
- viscosity: float32 [8, 8, 4, 1024], P('gx', 'gy', 'gz'), may hold values from 0.2 to 2
- occupied: int32 [8, 8, 4, 1024], P('gx', 'gy', 'gz'), may hold values 0 or 1
- base_viscosity: float32 [128, 256, 512], P('gx', 'gy', 'gz'), may hold values from 0.5 to 2
- pair_local: int32 [8, 8, 4, 4096], P('gx', 'gy', 'gz'), may hold values from 0 to 1023
- pair_owner: int32 [8, 8, 4, 4096], P('gx', 'gy', 'gz'), may hold values from 0 to 26
- pair_partner: int32 [8, 8, 4, 4096], P('gx', 'gy', 'gz'), may hold values from 0 to 1023
- pair_slot_mask: int32 [8, 8, 4, 4096], P('gx', 'gy', 'gz'), may hold values 0 or 1
Outputs:
- velocity_field: float32 [3, 128, 256, 512], P(None, 'gx', 'gy', 'gz')
- sphere_velocity: float32 [3, 8, 8, 4, 1024], P(None, 'gx', 'gy', 'gz')
Inputs may be any that keep to these rules, and one draw needn't show every extreme that they name: `cell_index`: row 0 is below 16, row 1 below 32, row 2 below 128.
All inputs are finite; a program needn't handle non-finite values. No bound on the sum of `occupied` or of `pair_slot_mask` on one device may be relied on, other than what follows from the above.
Results may differ from a plain program's by a relative error of at most 0.0003.
Values sent between devices are 32-bit elements; how exact they have to be, the bound alone decides.
A program may use at most 128 MiB of HBM per device.

v0:
```python
import functools
import jax
import jax.numpy as jnp
from jax import lax
from jax.experimental import pallas as pl
from jax.experimental.pallas import tpu as pltpu
from jax.sharding import PartitionSpec as P

spread_sigma = 0.8
damping = 0.5
lubrication_strength = 8.0
minimum_gap = 4.0
sharpness = 1.0 / (2.0 * spread_sigma * spread_sigma)

CX, CY, CZ = 16, 32, 128
SLOTS = 1024
PAIRS = 4096
TILES = 3 * PAIRS // 128
QB = 1024
REACH = 5
PLANES = 28
ROWS = 48
ROW0 = 5
BF = jnp.bfloat16
F32 = jnp.float32
NT = (((1,), (1,)), ((), ()))
NN = (((1,), (0,)), ((), ()))
TN = (((0,), (0,)), ((), ()))


def halves(value):
    high = value.astype(BF)
    return high, (value - high.astype(F32)).astype(BF)


def dot(a, b, dims):
    return lax.dot_general(a, b, dims, preferred_element_type=F32)


def dot3(a, b, dims):
    return dot(a[0], b[0], dims) + dot(a[1], b[0], dims) + dot(a[0], b[1], dims)


def iota(shape, dim):
    return lax.broadcasted_iota(jnp.int32, shape, dim)


def roll(value, shift, axis):
    shift = shift % value.shape[axis]
    return pltpu.roll(value, shift, axis) if shift else value


def lanes(value, index):
    return jnp.take_along_axis(value, jnp.broadcast_to(index, value.shape), axis=1)


def gauss(shift, offset):
    t = shift + 0.5 - offset
    return jnp.exp(-(t * t) * sharpness)


def norm(offset):
    total = gauss(-2.0, offset)
    for k in range(-1, 3):
        total = total + gauss(float(k), offset)
    return total


def window(cells, target, offset):
    shift = target.astype(F32) - cells
    return jnp.where(jnp.abs(shift) <= 2.0, gauss(shift, offset), 0.0)


def hot_rows(q, hot_p, hot_a, l):
    rows = iota((256, 128), 0)

    def tile(t, carry):
        for j in range(4):
            n = t * 4 + j
            at = pl.multiple_of(n * 128, 128)
            par = q[l, 2, pl.ds(n, 1), :] % 256
            loc = q[l, 0, pl.ds(n, 1), :] % 256
            hot_p[l, :, pl.ds(at, 128)] = jnp.where(rows == par, 1.0, 0.0).astype(BF)
            hot_a[l, :, pl.ds(at, 128)] = jnp.where(rows == loc, 1.0, 0.0).astype(BF)
        return carry

    lax.fori_loop(0, PAIRS // 512, tile, 0)


def split_rows(v, ref, at):
    high, low = halves(v)
    ref[at, 0:256] = high
    ref[at, 256:512] = low


def row_of(q, l, j, ch):
    n = QB // 128
    return jnp.concatenate([q[l, j, pl.ds(ch * n + t, 1), :] for t in range(n)], axis=1)


def pick(found, slab, count):
    wide = jnp.broadcast_to(slab, (8, QB))
    out = found[0:8]
    for k in range(1, count):
        out = jnp.where(wide == k, found[k * 8:(k + 1) * 8], out)
    return out


def keep(out, ref, l, ch):
    n = QB // 128
    for t in range(n):
        ref[l * (PAIRS // 128) + ch * n + t] = out[:, t * 128:(t + 1) * 128]


def find_mine(src, q, hot_a, mtab, mine, l):
    for h in range(2):
        split_rows(jnp.concatenate([src[2 * h], src[2 * h + 1]], axis=0), mtab, pl.ds(h * 16, 16))

    def step(ch, carry):
        hot = hot_a[l, :, pl.ds(pl.multiple_of(ch * QB, QB), QB)]
        found = dot(mtab[:, 0:256], hot, NN) + dot(mtab[:, 256:512], hot, NN)
        keep(pick(found, row_of(q, l, 0, ch) // 256, 4), mine, l, ch)
        return carry

    lax.fori_loop(0, PAIRS // QB, step, 0)


def codes(own):
    one = lambda c: jnp.where(c, 1, 0)
    dx = one(own >= 9) + one(own >= 18)
    rest = own - 9 * dx
    dy = one(rest >= 3) + one(rest >= 6)
    return dx, dy, rest - 3 * dy


def find_others(s, q, hot_p, tab, other):
    def fill(n, carry):
        v = jnp.concatenate([s[n // 2, n % 2 * 2], s[n // 2, n % 2 * 2 + 1]], axis=0)
        split_rows(v, tab, pl.ds(pl.multiple_of(n * 16, 16), 16))
        return carry

    lax.fori_loop(0, 18, fill, 0)

    def step(it, carry):
        l = it // (PAIRS // QB)
        ch = it % (PAIRS // QB)
        hot = hot_p[l, :, pl.ds(pl.multiple_of(ch * QB, QB), QB)]
        dx, dy, _ = codes(row_of(q, l, 1, ch))
        slab = (dy * 3 + dx) * 4 + row_of(q, l, 2, ch) // 256
        found = dot(tab[:, 0:256], hot, NN) + dot(tab[:, 256:512], hot, NN)
        keep(pick(found, slab, 36), other, l, ch)
        return carry

    lax.fori_loop(0, 3 * PAIRS // QB, step, 0)


def push_forces(q, mine, other, push, keys):
    for l in range(3):
        at = slice(l * (PAIRS // 128), (l + 1) * (PAIRS // 128))
        loc, own, par, live = (q[l, j] for j in range(4))
        dx, dy, dz = codes(own)
        m = [mine[at, r, :] for r in range(8)]
        o = [other[at, r, :] for r in range(8)]
        r = [
            (o[c] - m[c]) + (o[3 + c] - m[3 + c]) + (code - 1).astype(F32) * float(side)
            for c, (code, side) in enumerate(((dx, CX), (dy, CY), (dz, CZ)))
        ]
        spacing = jnp.sqrt(r[0] * r[0] + r[1] * r[1] + r[2] * r[2])
        clearance = spacing - m[6] - o[6]
        want = (1, 2, 0)[l]
        weight = (
            jnp.where(dz == want, live, 0).astype(F32) * m[7] * o[7] * lubrication_strength
            / (jnp.maximum(spacing, 1.0) * jnp.maximum(clearance, minimum_gap))
        )
        for c in range(3):
            v = r[c] * weight
            high = v.astype(BF).astype(F32)
            push[c, at] = high
            push[3 + c, at] = v - high
        keys[0, at] = (dy * 3 + dx) * 4 + par // 256
        keys[1, at] = loc // 256


def sum_forces(push, keys, hot_p, hot_a, acc, selves):
    acc[...] = jnp.zeros_like(acc)
    selves[...] = jnp.zeros_like(selves)
    n = QB // 128

    def step(it, carry):
        l = it // (PAIRS // QB)
        ch = it % (PAIRS // QB)
        at = pl.multiple_of(ch * QB, QB)

        def spread_rows(which, count):
            cols = []
            for t in range(n):
                k = it * n + t
                hit = iota((count, 128), 0) == keys[which, pl.ds(k, 1), :]
                cols.append(jnp.concatenate([jnp.where(hit, push[p, pl.ds(k, 1), :], 0.0) for p in range(6)], axis=0).astype(BF))
            return jnp.concatenate(cols, axis=1)

        sums = dot(spread_rows(0, 40), hot_p[l, :, pl.ds(at, QB)], NT)
        acc[...] -= (sums[0:120] + sums[120:240]).reshape(3, 40, 256)
        sums = dot(spread_rows(1, 8), hot_a[l, :, pl.ds(at, QB)], NT)
        selves[l] += sums[0:24] + sums[24:48]
        return carry

    lax.fori_loop(0, 3 * PAIRS // QB, step, 0)


X0 = (0, 3, 19)
NXS = (7, 20, 7)
R0 = (0, 0, 34)


def edge_rows():
    line = iota((128, 1), 0)
    k = line % 8
    low = line // 32 % 2 == 0
    kept = jnp.where(low, -5 + k, 125 + k)
    sent = jnp.where(low, -3 + k, 123 + k)
    return jnp.where(line < 64, kept, sent), line // 8 % 4


def axis_tables(s, b, kc, dx, dy, x0, nx, r0, ny):
    v = s[b, kc]
    offs = [v[3 + c:4 + c] for c in range(3)]
    dx_cells = jnp.asarray(dx * CX, jnp.int32).astype(F32)
    wx = window(v[0:1] + dx_cells, iota((nx, 256), 0) + (x0 - REACH), offs[0])
    wy = window(v[1:2] + float(dy * CY), iota((ny, 256), 0) + (r0 - ROW0), offs[1])
    wx = wx / (norm(offs[0]) * norm(offs[1]) * norm(offs[2]))
    wz = window(v[2:3], iota((128, 256), 0), offs[2])
    wedge = window(v[2:3], edge_rows()[0], offs[2])
    return wx, wy, jnp.concatenate([wz, wedge], axis=0)


def long_tables(s, b, dx, x0, nx, ph, pw, zt):
    def chunk(kc, carry):
        wx, wy, z = axis_tables(s, b, kc, dx, 0, x0, nx, 0, 40)
        at = pl.ds(pl.multiple_of(kc * 256, 256), 256)
        for x in range(nx):
            high, low = halves(wx[x:x + 1] * wy)
            ph[x * 40:(x + 1) * 40, at] = high
            pw[x * 40:(x + 1) * 40, at] = low
        zt[:, at] = z
        return carry

    lax.fori_loop(0, 4, chunk, 0)


def short_tables(s, b, dx, dy, x0, nx, pf, zh, zl):
    def chunk(kc, carry):
        wx, wy, z = axis_tables(s, b, kc, dx, dy, x0, nx, R0[dy + 1], 8)
        at = pl.ds(pl.multiple_of(kc * 256, 256), 256)
        for x in range(nx):
            pf[x * 8:(x + 1) * 8, at] = wx[x:x + 1] * wy
        high, low = halves(z)
        zh[:, at] = high
        zl[:, at] = low
        return carry

    lax.fori_loop(0, 4, chunk, 0)


def line_of(ref, b, c):
    return jnp.concatenate([ref[b, c * 4 + h:c * 4 + h + 1, :] for h in range(4)], axis=1)


def long_brick(ph, pw, zt, load, parts, main, edge, x0, nx):
    comp = edge_rows()[1]
    cols = []
    for part in parts:
        if part is None:
            v = jnp.zeros((128, SLOTS), F32)
            for c, value in load.items():
                v = jnp.where(comp == c, value, v)
            cols.append(zt[128:256, :] * v)
        else:
            cols.append(zt[0:128, :] * load[part])
    res = dot3((ph[...], pw[...]), halves(jnp.concatenate(cols, axis=0)), NT).reshape(nx, 40, 256)
    for n, part in enumerate(parts):
        here = res[:, :, n * 128:(n + 1) * 128]
        if part is None:
            edge[pl.ds(x0, nx), 0:40, :] += here
        else:
            main[part, pl.ds(x0, nx), 0:40, :] += here


def short_brick(pf, zh, zl, load, main, edge, x0, nx, r0):
    lane = iota((nx, 8, 128), 2)
    value = jnp.concatenate([pf[...] * v for v in load.values()], axis=0)
    res = dot3(halves(value), (zh[...], zl[...]), NT).reshape(len(load), nx, 8, 256)
    rim = jnp.zeros((nx, 8, 128), F32)
    for n, c in enumerate(load):
        main[c, pl.ds(x0, nx), r0:r0 + 8, :] += res[n, :, :, 0:128]
        rim = jnp.where(lane // 8 % 4 == c, res[n, :, :, 128:256], rim)
    edge[pl.ds(x0, nx), r0:r0 + 8, :] += rim


def assemble_base(bx, by, i):
    rows = jnp.concatenate([by[0, i], bx[i], by[1, i]], axis=0)
    return roll(rows, ROW0 - 8, 0)


def wrap_rims(bx, by, main, edge, pack):
    lane = iota((ROWS, 128), 1)
    within = [(29, 32, 0), (56, 59, 125), (91, 96, 0), (120, 125, 123)]
    index = lane
    mask = lane < 0
    for first, last, z in within:
        inside = (lane >= first) & (lane < last)
        index = jnp.where(inside, lane - first + z, index)
        mask = mask | inside

    def wrap(g, carry):
        tiles = []
        for j in range(4):
            i = g * 4 + j
            b = assemble_base(bx, by, i)
            main[3, i] += b
            t = edge[i] + jnp.where(mask, lanes(b, index), 0.0)
            edge[i] = t
            tiles.append(t)
        for side in range(2):
            out = jnp.zeros((ROWS, 128), F32)
            for j in range(4):
                out = jnp.where(lane // 32 == j, roll(tiles[j], 32 * j - 64 - 32 * side, 1), out)
            pack[side, g] = out
        return carry

    lax.fori_loop(0, PLANES // 4, wrap, 0)


def first_sweep(main, edge, rim, ua, ha, inv, hvisco, hinv):
    lane = iota((ROWS, 128), 1)
    thick = lane // 32 * 32 + 24 + lane % 8

    def start(g, carry):
        from_low, from_high = rim[0, g], rim[1, g]
        for j in range(4):
            i = g * 4 + j
            got = jnp.where(lane < 32, roll(from_low, -32 * j, 1), 0.0)
            got = jnp.where(lane // 32 == 1, roll(from_high, 32 - 32 * j, 1), got)
            total = jnp.where(lane < 64, edge[i], 0.0) + got
            v = lanes(total, thick)
            r = 1.0 / (damping + 6.0 * v)
            hvisco[i] = v
            hinv[i] = r
            edge[i] = total
            ha[i] = total * r
            m = []
            for c in range(4):
                near = lanes(got, jnp.where(lane < 64, lane + (c * 8 + 5), lane + (33 + c * 8 - 126)) % 128)
                m.append(main[c, i] + jnp.where((lane < 2) | (lane >= 126), near, 0.0))
            main[3, i] = m[3]
            r = 1.0 / (damping + 6.0 * m[3])
            inv[i] = r
            for c in range(3):
                main[c, i] = m[c]
                ua[c, i] = m[c] * r
        return carry

    lax.fori_loop(0, PLANES // 4, start, 0)


def sweep(src, dst, hsrc, hdst, main, edge, inv, hvisco, hinv, first, rows):
    lane = iota((rows, 128), 1)
    at = slice(0, rows)

    def next_row(value, ref, *lead):
        return ref[(*lead, slice(1, rows + 1))] if rows < ROWS else roll(value, -1, 0)

    def plane(i, carry):
        h = hsrc[i, at]
        beside = hsrc[i - 1, at] + hsrc[i + 1, at] + roll(h, 1, 0) + next_row(h, hsrc, i) + roll(h, 1, 1) + roll(h, -1, 1)
        hdst[i, at] = (edge[i, at] + hvisco[i, at] * beside) * hinv[i, at]
        v, r = main[3, i, at], inv[i, at]
        for c in range(3):
            u = src[c, i, at]
            rim = lanes(h, jnp.where(lane == 0, c * 8 + 4, 35 + c * 8))
            before = jnp.where(lane == 0, rim, roll(u, 1, 1))
            after = jnp.where(lane == 127, rim, roll(u, -1, 1))
            beside = src[c, i - 1, at] + src[c, i + 1, at] + roll(u, 1, 0) + next_row(u, src, c, i) + before + after
            dst[c, i, at] = (main[c, i, at] + v * beside) * r
        return carry

    lax.fori_loop(first, 26 - first, plane, 0, unroll=4)


def interpolate(ub, hb, ph, pw, zt, s, uh, ul, out):
    for x in range(20):
        row = jnp.concatenate([ub[0, x + 3, 0:40], ub[1, x + 3, 0:40], ub[2, x + 3, 0:40], hb[x + 3, 0:40]], axis=1)
        high, low = halves(row)
        uh[x * 40:(x + 1) * 40] = high
        ul[x * 40:(x + 1) * 40] = low
    z, comp = edge_rows()
    line = iota((128, 1), 0)
    outside = ((z < 0) | (z >= CZ)) & (line < 64)

    def chunk(pc, carry):
        at = pl.ds(pl.multiple_of(pc * 256, 256), 256)
        res = dot3((uh[...], ul[...]), (ph[:, at], pw[:, at]), TN)
        wz = zt[0:128, at]
        rim = jnp.where(outside, zt[128:256, at] * res[384:512], 0.0)
        alive = s[4, pc, 7:8, :]
        for c in range(3):
            value = jnp.sum(res[c * 128:(c + 1) * 128] * wz + jnp.where(comp == c, rim, 0.0), axis=0, keepdims=True)
            out[c, pl.ds(2 * pc, 1), :] = (value * alive)[:, 0:128]
            out[c, pl.ds(2 * pc + 1, 1), :] = (value * alive)[:, 128:256]
        return carry

    lax.fori_loop(0, 4, chunk, 0)


def step_kernel(
    cell_in, offset_in, radius_in, force_in, visc_in, live_in, base_in,
    local_in, owner_in, partner_in, mask_in,
    field_out, vel_out,
    cell, offset, radius, force, visc, alive,
    s, thick, zs, q, hot_p, hot_a, tab, mtab, mine, other, push, keys, acc, selves,
    ry, rz, xs, rx1, rx2, loads,
    ph0, pw0, ph1, pw1, zt, pfy, pfd, zh, zl,
    bx, by, main, edge, pack, rim,
    ua, ub, ha, hb, inv, hvisco, hinv, uh, ul, vel,
    in_sem, send_sem, recv_sem, out_sem,
):
    me = {a: lax.axis_index(a) for a in ("gx", "gy", "gz")}

    def near(axis, step):
        n = lax.axis_size(axis)
        return {axis: lax.rem(me[axis] + step + n, n)}

    inputs = [
        (cell_in, cell), (offset_in, offset), (radius_in, radius), (force_in, force), (visc_in, visc),
        (live_in, alive), (base_in, bx.at[pl.ds(REACH, CX)]), (local_in, q.at[0, 0]), (owner_in, q.at[0, 1]),
        (partner_in, q.at[0, 2]), (mask_in, q.at[0, 3]),
    ]
    inputs = [pltpu.make_async_copy(a, b, in_sem.at[n]) for n, (a, b) in enumerate(inputs)]
    for c in inputs:
        c.start()

    barrier = pltpu.get_barrier_semaphore()
    greeted = [("gx", 1), ("gx", -1), ("gx", 2), ("gx", -2), ("gy", 1), ("gy", -1), ("gz", 1), ("gz", -1)]
    for axis, step in greeted:
        pl.semaphore_signal(barrier, inc=1, device_id=near(axis, step), device_id_type=pl.DeviceIdType.MESH)

    count = [0]

    def copy(src, dst, axis, step):
        n = count[0]
        count[0] += 1
        return pltpu.make_async_remote_copy(
            src_ref=src, dst_ref=dst, send_sem=send_sem.at[n], recv_sem=recv_sem.at[n],
            device_id=near(axis, step), device_id_type=pl.DeviceIdType.MESH,
        )

    three, low3, high3 = pl.ds(3, 3), pl.ds(0, 3), pl.ds(6, 3)
    s_x = [copy(s.at[4], s.at[3], "gx", 1), copy(s.at[4], s.at[5], "gx", -1)]
    s_x += [copy(thick.at[4], thick.at[3], "gx", 1), copy(thick.at[4], thick.at[5], "gx", -1)]
    s_y = [copy(s.at[three], s.at[low3], "gy", 1), copy(s.at[three], s.at[high3], "gy", -1)]
    s_y += [copy(thick.at[three], thick.at[low3], "gy", 1), copy(thick.at[three], thick.at[high3], "gy", -1)]
    s_z = [copy(s.at[4], zs.at[0], "gz", 1), copy(s.at[4], zs.at[1], "gz", -1)]
    q_z = [copy(q.at[0], q.at[1], "gz", 1), copy(q.at[0], q.at[2], "gz", -1)]
    b_x = [
        copy(bx.at[pl.ds(CX, REACH)], bx.at[pl.ds(0, REACH)], "gx", 1),
        copy(bx.at[pl.ds(REACH, REACH)], bx.at[pl.ds(CX + REACH, REACH)], "gx", -1),
    ]
    b_y = [
        copy(bx.at[:, pl.ds(CY - 8, 8)], by.at[0], "gy", 1),
        copy(bx.at[:, pl.ds(0, 8)], by.at[1], "gy", -1),
    ]
    a_y = [copy(acc.at[:, pl.ds(24, 16)], ry.at[0], "gy", 1), copy(acc.at[:, pl.ds(0, 16)], ry.at[1], "gy", -1)]
    a_z = [copy(selves.at[1], rz.at[0], "gz", -1), copy(selves.at[2], rz.at[1], "gz", 1)]
    a_x = [
        copy(xs.at[pl.ds(1, 2)], rx1.at[0], "gx", 1), copy(xs.at[pl.ds(0, 2)], rx1.at[1], "gx", -1),
        copy(xs.at[2], rx2.at[0], "gx", 2), copy(xs.at[0], rx2.at[1], "gx", -2),
    ]
    l_y = [copy(loads.at[three], loads.at[low3], "gy", 1), copy(loads.at[three], loads.at[high3], "gy", -1)]
    e_z = [copy(pack.at[0], rim.at[1], "gz", -1), copy(pack.at[1], rim.at[0], "gz", 1)]

    def start(copies):
        for c in copies:
            c.start()

    def arrived(copies):
        for c in copies:
            c.wait_recv()

    for c in inputs:
        c.wait()
    flags = alive[...].astype(F32)
    rows = [cell[c].astype(F32) for c in range(3)] + [offset[c] for c in range(3)] + [radius[...], flags]
    for r, v in enumerate(rows):
        for h in range(4):
            s[4, h, r:r + 1, 0:128] = v[2 * h:2 * h + 1]
            s[4, h, r:r + 1, 128:256] = v[2 * h + 1:2 * h + 2]
    thick[4] = visc[...] * flags
    pl.semaphore_wait(barrier, len(greeted))
    start(s_x)
    start(s_z)
    start(q_z)

    bx[26:28] = jnp.zeros((2, CY, CZ), F32)
    hot_rows(q, hot_p, hot_a, 0)
    find_mine(s.at[4], q, hot_a, mtab, mine, 0)
    arrived(s_z)
    arrived(q_z)
    for l in (1, 2):
        hot_rows(q, hot_p, hot_a, l)
        find_mine(zs.at[l - 1], q, hot_a, mtab, mine, l)
    arrived(s_x)
    start(s_y)
    main[...] = jnp.zeros_like(main)
    edge[...] = jnp.zeros_like(edge)
    long_tables(s, 4, 0, 3, 20, ph0, pw0, zt.at[0])
    arrived(s_y)
    start(b_x)

    find_others(s, q, hot_p, tab, other)
    push_forces(q, mine, other, push, keys)
    sum_forces(push, keys, hot_p, hot_a, acc, selves)

    start(a_y)
    start(a_z)
    def side_tables(it, carry):
        long_tables(s, 3 + 2 * it, 2 * it - 1, it * 19, 7, ph1.at[it], pw1.at[it], zt.at[1 + it])
        return carry

    lax.fori_loop(0, 2, side_tables, 0)
    arrived(a_y)
    arrived(a_z)
    xs[...] = jnp.zeros_like(xs)
    for c in range(3):
        middle = acc[c, 12:24] + ry[0, c, 0:12] + ry[1, c, 0:12]
        f = force[c]
        f = jnp.concatenate(
            [jnp.concatenate([f[2 * h:2 * h + 1], f[2 * h + 1:2 * h + 2]], axis=1) for h in range(4)], axis=0
        )
        at = slice(c * 8, c * 8 + 4)
        f = f + selves[0, at] + rz[0, at] + rz[1, at]
        xs[0, c * 4:c * 4 + 4] = middle[0:4]
        xs[1, c * 4:c * 4 + 4] = middle[4:8] + f
        xs[2, c * 4:c * 4 + 4] = middle[8:12]
    start(a_x)
    for n, dy in enumerate((-1, 1)):
        short_tables(s, 3 * (dy + 1) + 1, 0, dy, 3, 20, pfy.at[n], zh.at[n * 3], zl.at[n * 3])

        def corner(it, carry):
            k = n * 3 + 1 + it
            short_tables(s, 3 * (dy + 1) + 2 * it, 2 * it - 1, dy, it * 19, 7, pfd.at[n * 2 + it], zh.at[k], zl.at[k])
            return carry

        lax.fori_loop(0, 2, corner, 0)

    def thickness(b):
        return {3: jnp.concatenate([thick[b, t:t + 1, :] for t in range(8)], axis=1)}

    def short_all(load):
        for n, dy in enumerate((-1, 1)):
            k = n * 3
            short_brick(pfy[n], zh.at[k], zl.at[k], load(3 * (dy + 1) + 1), main, edge, 3, 20, R0[dy + 1])

            def corner(it, carry):
                k = n * 3 + 1 + it
                b = 3 * (dy + 1) + 2 * it
                short_brick(pfd[n * 2 + it], zh.at[k], zl.at[k], load(b), main, edge, it * 19, 7, R0[dy + 1])
                return carry

            lax.fori_loop(0, 2, corner, 0)

    def long_all(load, parts):
        long_brick(ph0, pw0, zt.at[0], load(4), parts, main, edge, 3, 20)

        def side(it, carry):
            long_brick(ph1.at[it], pw1.at[it], zt.at[1 + it], load(3 + 2 * it), parts, main, edge, it * 19, 7)
            return carry

        lax.fori_loop(0, 2, side, 0)

    long_all(thickness, (3, None))
    short_all(thickness)

    arrived(a_x)
    for n in range(3):
        if n == 0:
            total = rx1[0, 0] + rx2[0] + xs[0]
        elif n == 1:
            total = xs[1] + rx1[0, 1] + rx1[1, 0]
        else:
            total = rx1[1, 1] + rx2[1] + xs[2]
        for h in range(4):
            on = s[3 + n, h, 7:8, :]
            for c in range(3):
                loads[3 + n, c * 4 + h:c * 4 + h + 1, :] = on * total[c * 4 + h:c * 4 + h + 1]
        loads[3 + n, 12:16] = jnp.zeros((4, 256), F32)
    start(l_y)
    arrived(b_x)
    start(b_y)

    def forces(b):
        return {c: line_of(loads, b, c) for c in range(3)}

    long_all(forces, (2, None))
    arrived(l_y)
    short_all(forces)
    arrived(b_y)
    wrap_rims(bx, by, main, edge, pack)
    start(e_z)
    long_all(forces, (0, 1))
    arrived(e_z)

    first_sweep(main, edge, rim, ua, ha, inv, hvisco, hinv)
    rest = (main, edge, inv, hvisco, hinv)
    sweep(ua, ub, ha, hb, *rest, 1, 48)
    sweep(ub, ua, hb, ha, *rest, 2, 40)
    sweep(ua, ub, ha, hb, *rest, 3, 40)

    def finish(x, carry):
        for c in range(3):
            ua[c, x, 0:CY] = ub[c, x + REACH, ROW0:ROW0 + CY, :]
        return carry

    lax.fori_loop(0, CX, finish, 0)
    outputs = [pltpu.make_async_copy(ua.at[:, pl.ds(0, CX), pl.ds(0, CY)], field_out, out_sem.at[0])]
    outputs[0].start()
    interpolate(ub, hb, ph0, pw0, zt.at[0], s, uh, ul, vel)
    outputs.append(pltpu.make_async_copy(vel, vel_out, out_sem.at[1]))
    outputs[1].start()
    for group in (s_x, s_y, s_z, q_z, b_x, b_y, a_y, a_z, a_x, l_y, e_z):
        for c in group:
            c.wait_send()
    for c in outputs:
        c.wait()


def scratch():
    f = lambda *shape: pltpu.VMEM(shape, F32)
    i = lambda *shape: pltpu.VMEM(shape, jnp.int32)
    b = lambda *shape: pltpu.VMEM(shape, BF)
    grid = lambda *lead: pltpu.VMEM(lead + (PLANES, ROWS, 128), F32)
    sem = pltpu.SemaphoreType.DMA
    return [
        i(3, 8, 128), f(3, 8, 128), f(8, 128), f(3, 8, 128), f(8, 128), i(8, 128),
        f(9, 4, 8, 256), f(9, 8, 128), f(2, 4, 8, 256), i(3, 4, 32, 128),
        b(3, 256, PAIRS), b(3, 256, PAIRS), b(288, 512), b(32, 512),
        f(TILES, 8, 128), f(TILES, 8, 128), f(6, TILES, 128), i(2, TILES, 128),
        f(3, 40, 256), f(3, 24, 256),
        f(2, 3, 16, 256), f(2, 24, 256), f(3, 16, 256), f(2, 2, 16, 256), f(2, 16, 256), f(9, 16, 256),
        b(800, SLOTS), b(800, SLOTS), b(2, 280, SLOTS), b(2, 280, SLOTS), f(3, 256, SLOTS),
        f(2, 160, SLOTS), f(4, 56, SLOTS), b(6, 256, SLOTS), b(6, 256, SLOTS),
        f(PLANES, CY, CZ), f(2, PLANES, 8, CZ), grid(4), grid(), f(2, PLANES // 4, ROWS, 128), f(2, PLANES // 4, ROWS, 128),
        grid(3), grid(3), grid(), grid(), grid(), grid(), grid(), b(800, 512), b(800, 512), f(3, 8, 128),
        sem((11,)), sem((28,)), sem((28,)), sem((2,)),
    ]


def body(
    cell_index, cell_offset, radius, forcing, viscosity, occupied, base_viscosity,
    pair_local, pair_owner, pair_partner, pair_slot_mask,
):
    args = [a.reshape(3, 8, 128) if a.shape[0] == 3 else a.reshape(8, 128) for a in (
        cell_index, cell_offset, radius, forcing, viscosity, occupied
    )]
    args += [base_viscosity]
    args += [a.reshape(32, 128) for a in (pair_local, pair_owner, pair_partner, pair_slot_mask)]
    field, velocity = pl.pallas_call(
        step_kernel,
        out_shape=(
            jax.ShapeDtypeStruct((3, CX, CY, CZ), F32),
            jax.ShapeDtypeStruct((3, 8, 128), F32),
        ),
        in_specs=[pl.BlockSpec(memory_space=pltpu.HBM)] * 11,
        out_specs=(pl.BlockSpec(memory_space=pltpu.HBM),) * 2,
        scratch_shapes=scratch(),
        compiler_params=pltpu.CompilerParams(
            collective_id=0, has_side_effects=True, vmem_limit_bytes=62 * 2**20
        ),
        name="coupling",
    )(*args)
    return field, velocity.reshape(3, 1, 1, 1, SLOTS)


def solution(mesh):
    line = P("gx", "gy", "gz", None)
    wide = P(None, "gx", "gy", "gz", None)
    placed = (wide, wide, line, wide, line, line, P("gx", "gy", "gz"), line, line, line, line)
    return jax.shard_map(
        body,
        mesh=mesh,
        in_specs=placed,
        out_specs=(P(None, "gx", "gy", "gz"), wide),
        check_vma=False,
    )
```

profile of v0, /device:TPU:1, one launch (start us, length us, event | category | flops | bytes accessed | tf_op | source)
XLA Modules:
  0.0 83.7 jit_solution(11250538453518741133)
XLA Ops:
  0.6 80.4 %coupling.1 = (f32[3,16,32,128]{3,2,1,0:T(8,128)}, f32[3,8,128]{2,1,0:T(8,128)}) custom-call(s32[3,8,128]{2,1,0:T(8,128)} %bitcast.15, f32[3,8,128]{2,1,0:T(8,128)} %bitcast.16, f32[8,128]{1,0:T(8,128)} %bitcast.19, f32[3,8,128]{2,1,0:T(8,128)} %bitcast.17, f32[8,128]{1,0:T(8,128)} %bitcast.20, s32[8,128]{1,0:T(8,128)} %bitcast.21, f32[16,32,128]{2,1,0:T(8,128)} %base_in.1, ...), custom_call_target="tpu_custom_call" | custom-call | tf_op jit(solution)/shard_map/coupling/pallas_call | solution.py:666
  81.0 0.0 copy-start
  81.1 2.1 %copy.17 = f32[3,16,32,128]{3,2,1,0:T(8,128)} copy(f32[3,16,32,128]{3,2,1,0:T(8,128)} %get-tuple-element.12) | data formatting | bytes 1572864
  83.1 0.0 copy-done
  83.1 0.6 copy.18
Async XLA Ops:
  81.0 2.1 %copy-start = (f32[3,8,128]{2,1,0:T(8,128)S(1)}, f32[3,8,128]{2,1,0:T(8,128)}, u32[]{:S(2)}) copy-start(f32[3,8,128]{2,1,0:T(8,128)} %get-tuple-element.5) | copy-start | bytes 36868
where the time goes:
time: 85.1 us; the launch traced here: 83.7 us
  Pallas kernels  80.4 us (94%)
  local copies, waits for them, and re-layouts  2.67 us (3%)
    pallas_call x1, Pallas kernels, body(): pl.pallas_call(step_kernel, out_shape=(jax.ShapeDtypeStruct((3, CX, CY, C...  80.4 us
    unnamed x4, local copies, waits for them, and re-layouts  2.67 us

commit v1 on v0

--- a/solution.py
+++ b/solution.py
@@ -51,7 +51,8 @@
 
 
 def lanes(value, index):
-    return jnp.take_along_axis(value, jnp.broadcast_to(index, value.shape), axis=1)
+    index = jnp.broadcast_to(index, value.shape)
+    return jnp.take_along_axis(value, index, axis=1, mode="promise_in_bounds")
 
 
 def gauss(shift, offset):
@@ -78,19 +79,13 @@
         for j in range(4):
             n = t * 4 + j
             at = pl.multiple_of(n * 128, 128)
-            par = q[l, 2, pl.ds(n, 1), :] % 256
-            loc = q[l, 0, pl.ds(n, 1), :] % 256
+            par = q[l, 2, pl.ds(n, 1), :] & 255
+            loc = q[l, 0, pl.ds(n, 1), :] & 255
             hot_p[l, :, pl.ds(at, 128)] = jnp.where(rows == par, 1.0, 0.0).astype(BF)
             hot_a[l, :, pl.ds(at, 128)] = jnp.where(rows == loc, 1.0, 0.0).astype(BF)
         return carry
 
     lax.fori_loop(0, PAIRS // 512, tile, 0)
-
-
-def split_rows(v, ref, at):
-    high, low = halves(v)
-    ref[at, 0:256] = high
-    ref[at, 256:512] = low
 
 
 def row_of(q, l, j, ch):
@@ -98,31 +93,26 @@
     return jnp.concatenate([q[l, j, pl.ds(ch * n + t, 1), :] for t in range(n)], axis=1)
 
 
-def pick(found, slab, count):
+def pick(found, slab, slabs, out):
     wide = jnp.broadcast_to(slab, (8, QB))
-    out = found[0:8]
-    for k in range(1, count):
-        out = jnp.where(wide == k, found[k * 8:(k + 1) * 8], out)
+    for n, k in enumerate(slabs):
+        out = jnp.where(wide == k, found[n * 8:(n + 1) * 8], out)
     return out
 
 
-def keep(out, ref, l, ch):
-    n = QB // 128
-    for t in range(n):
-        ref[l * (PAIRS // 128) + ch * n + t] = out[:, t * 128:(t + 1) * 128]
-
-
-def find_mine(src, q, hot_a, mtab, mine, l):
-    for h in range(2):
-        split_rows(jnp.concatenate([src[2 * h], src[2 * h + 1]], axis=0), mtab, pl.ds(h * 16, 16))
-
-    def step(ch, carry):
-        hot = hot_a[l, :, pl.ds(pl.multiple_of(ch * QB, QB), QB)]
-        found = dot(mtab[:, 0:256], hot, NN) + dot(mtab[:, 256:512], hot, NN)
-        keep(pick(found, row_of(q, l, 0, ch) // 256, 4), mine, l, ch)
-        return carry
-
-    lax.fori_loop(0, PAIRS // QB, step, 0)
+def find_mine(src, q, mine, l):
+    def step(t, carry):
+        for j in range(4):
+            n = t * 4 + j
+            loc = jnp.broadcast_to(q[l, 0, pl.ds(n, 1), :], (8, 128))
+            index, block = loc & 127, loc >> 7
+            out = jnp.zeros((8, 128), F32)
+            for k in range(8):
+                out = jnp.where(block == k, lanes(src[k // 2, :, k % 2 * 128:k % 2 * 128 + 128], index), out)
+            mine[l * (PAIRS // 128) + n] = out
+        return carry
+
+    lax.fori_loop(0, PAIRS // 512, step, 0)
 
 
 def codes(own):
@@ -133,25 +123,37 @@
     return dx, dy, rest - 3 * dy
 
 
-def find_others(s, q, hot_p, tab, other):
-    def fill(n, carry):
-        v = jnp.concatenate([s[n // 2, n % 2 * 2], s[n // 2, n % 2 * 2 + 1]], axis=0)
-        split_rows(v, tab, pl.ds(pl.multiple_of(n * 16, 16), 16))
-        return carry
-
-    lax.fori_loop(0, 18, fill, 0)
+def find_others(s, q, hot_p, tab, other, bricks, first):
+    count = len(bricks)
+    def fill(brick, n):
+        v = jnp.concatenate([s[brick, 0], s[brick, 1], s[brick, 2], s[brick, 3]], axis=0)
+        high, low = halves(v)
+        tab[n * 32:(n + 1) * 32, 0:256] = high
+        tab[n * 32:(n + 1) * 32, 256:512] = low
+
+    for n, brick in enumerate(bricks):
+        fill(brick, n)
+    slabs = [b * 4 + h for b in bricks for h in range(4)]
+    tiles = QB // 128
 
     def step(it, carry):
         l = it // (PAIRS // QB)
         ch = it % (PAIRS // QB)
         hot = hot_p[l, :, pl.ds(pl.multiple_of(ch * QB, QB), QB)]
         dx, dy, _ = codes(row_of(q, l, 1, ch))
-        slab = (dy * 3 + dx) * 4 + row_of(q, l, 2, ch) // 256
-        found = dot(tab[:, 0:256], hot, NN) + dot(tab[:, 256:512], hot, NN)
-        keep(pick(found, slab, 36), other, l, ch)
-        return carry
-
-    lax.fori_loop(0, 3 * PAIRS // QB, step, 0)
+        slab = (dy * 3 + dx) * 4 + (row_of(q, l, 2, ch) >> 8)
+        rows = slice(0, count * 32)
+        found = dot(tab[rows, 0:256], hot, NN) + dot(tab[rows, 256:512], hot, NN)
+        if first:
+            out = jnp.zeros((8, QB), F32)
+        else:
+            out = jnp.concatenate([other[it * tiles + t] for t in range(tiles)], axis=1)
+        out = pick(found, slab, slabs, out)
+        for t in range(tiles):
+            other[it * tiles + t] = out[:, t * 128:(t + 1) * 128]
+        return carry
+
+    lax.fori_loop(0, 3 * PAIRS // QB, step, 0, unroll=2)
 
 
 def push_forces(q, mine, other, push, keys):
@@ -177,35 +179,43 @@
             high = v.astype(BF).astype(F32)
             push[c, at] = high
             push[3 + c, at] = v - high
-        keys[0, at] = (dy * 3 + dx) * 4 + par // 256
-        keys[1, at] = loc // 256
-
-
-def sum_forces(push, keys, hot_p, hot_a, acc, selves):
+        keys[0, at] = (dy * 3 + dx) * 4 + (par >> 8)
+        keys[1, at] = loc >> 8
+
+
+def spread_rows(push, keys, it, count):
+    cols = []
+    for t in range(QB // 128):
+        k = it * (QB // 128) + t
+        hit = iota((count, 128), 0) == keys[pl.ds(k, 1), :]
+        rows = [jnp.where(hit, push[p, pl.ds(k, 1), :], 0.0) for p in range(6)]
+        cols.append(jnp.concatenate(rows, axis=0).astype(BF))
+    return jnp.concatenate(cols, axis=1)
+
+
+def sum_others(push, keys, hot_p, acc):
     acc[...] = jnp.zeros_like(acc)
-    selves[...] = jnp.zeros_like(selves)
-    n = QB // 128
 
     def step(it, carry):
         l = it // (PAIRS // QB)
-        ch = it % (PAIRS // QB)
-        at = pl.multiple_of(ch * QB, QB)
-
-        def spread_rows(which, count):
-            cols = []
-            for t in range(n):
-                k = it * n + t
-                hit = iota((count, 128), 0) == keys[which, pl.ds(k, 1), :]
-                cols.append(jnp.concatenate([jnp.where(hit, push[p, pl.ds(k, 1), :], 0.0) for p in range(6)], axis=0).astype(BF))
-            return jnp.concatenate(cols, axis=1)
-
-        sums = dot(spread_rows(0, 40), hot_p[l, :, pl.ds(at, QB)], NT)
+        at = pl.multiple_of(it % (PAIRS // QB) * QB, QB)
+        sums = dot(spread_rows(push, keys.at[0], it, 40), hot_p[l, :, pl.ds(at, QB)], NT)
         acc[...] -= (sums[0:120] + sums[120:240]).reshape(3, 40, 256)
-        sums = dot(spread_rows(1, 8), hot_a[l, :, pl.ds(at, QB)], NT)
+        return carry
+
+    lax.fori_loop(0, 3 * PAIRS // QB, step, 0, unroll=2)
+
+
+def sum_mine(push, keys, hot_a, selves, l):
+    selves[l] = jnp.zeros((24, 256), F32)
+
+    def step(ch, carry):
+        it = l * (PAIRS // QB) + ch
+        sums = dot(spread_rows(push, keys.at[1], it, 8), hot_a[l, :, pl.ds(pl.multiple_of(ch * QB, QB), QB)], NT)
         selves[l] += sums[0:24] + sums[24:48]
         return carry
 
-    lax.fori_loop(0, 3 * PAIRS // QB, step, 0)
+    lax.fori_loop(0, PAIRS // QB, step, 0, unroll=2)
 
 
 X0 = (0, 3, 19)
@@ -228,21 +238,22 @@
     dx_cells = jnp.asarray(dx * CX, jnp.int32).astype(F32)
     wx = window(v[0:1] + dx_cells, iota((nx, 256), 0) + (x0 - REACH), offs[0])
     wy = window(v[1:2] + float(dy * CY), iota((ny, 256), 0) + (r0 - ROW0), offs[1])
-    wx = wx / (norm(offs[0]) * norm(offs[1]) * norm(offs[2]))
     wz = window(v[2:3], iota((128, 256), 0), offs[2])
-    wedge = window(v[2:3], edge_rows()[0], offs[2])
-    return wx, wy, jnp.concatenate([wz, wedge], axis=0)
+    eight = iota((8, 256), 0)
+    wedge = [window(v[2:3], eight + z, offs[2]) for z in (-5, 125, -3, 123)]
+    return wx, wy, wz, [w for w in wedge for c in range(4)]
 
 
 def long_tables(s, b, dx, x0, nx, ph, pw, zt):
     def chunk(kc, carry):
-        wx, wy, z = axis_tables(s, b, kc, dx, 0, x0, nx, 0, 40)
+        wx, wy, wz, wedge = axis_tables(s, b, kc, dx, 0, x0, nx, 0, 40)
         at = pl.ds(pl.multiple_of(kc * 256, 256), 256)
         for x in range(nx):
             high, low = halves(wx[x:x + 1] * wy)
             ph[x * 40:(x + 1) * 40, at] = high
             pw[x * 40:(x + 1) * 40, at] = low
-        zt[:, at] = z
+        zt[0:128, at] = wz
+        zt[128:256, at] = jnp.concatenate(wedge, axis=0)
         return carry
 
     lax.fori_loop(0, 4, chunk, 0)
@@ -250,16 +261,27 @@
 
 def short_tables(s, b, dx, dy, x0, nx, pf, zh, zl):
     def chunk(kc, carry):
-        wx, wy, z = axis_tables(s, b, kc, dx, dy, x0, nx, R0[dy + 1], 8)
+        wx, wy, wz, wedge = axis_tables(s, b, kc, dx, dy, x0, nx, R0[dy + 1], 8)
         at = pl.ds(pl.multiple_of(kc * 256, 256), 256)
         for x in range(nx):
             pf[x * 8:(x + 1) * 8, at] = wx[x:x + 1] * wy
-        high, low = halves(z)
-        zh[:, at] = high
-        zl[:, at] = low
+        high, low = halves(wz)
+        zh[0:128, at] = high
+        zl[0:128, at] = low
+        pairs = [jnp.concatenate(wedge[n:n + 2], axis=0) for n in (0, 4, 8, 12)]
+        for n, (high, low) in enumerate(halves(p) for p in pairs):
+            for k in range(2):
+                rows = slice(128 + n * 32 + k * 16, 128 + n * 32 + k * 16 + 16)
+                zh[rows, at] = high
+                zl[rows, at] = low
         return carry
 
     lax.fori_loop(0, 4, chunk, 0)
+
+
+def envelope_scale(s, b, h):
+    total = norm(s[b, h])
+    return 1.0 / (total[3:4] * total[4:5] * total[5:6])
 
 
 def line_of(ref, b, c):
@@ -302,7 +324,7 @@
     return roll(rows, ROW0 - 8, 0)
 
 
-def wrap_rims(bx, by, main, edge, pack):
+def wrap_rims(bx, by, edge, pack):
     lane = iota((ROWS, 128), 1)
     within = [(29, 32, 0), (56, 59, 125), (91, 96, 0), (120, 125, 123)]
     index = lane
@@ -317,7 +339,6 @@
         for j in range(4):
             i = g * 4 + j
             b = assemble_base(bx, by, i)
-            main[3, i] += b
             t = edge[i] + jnp.where(mask, lanes(b, index), 0.0)
             edge[i] = t
             tiles.append(t)
@@ -329,6 +350,16 @@
         return carry
 
     lax.fori_loop(0, PLANES // 4, wrap, 0)
+
+
+def add_base(bx, by, main):
+    def plane(g, carry):
+        for j in range(4):
+            i = g * 4 + j
+            main[3, i] += assemble_base(bx, by, i)
+        return carry
+
+    lax.fori_loop(0, PLANES // 4, plane, 0)
 
 
 def first_sweep(main, edge, rim, ua, ha, inv, hvisco, hinv):
@@ -387,29 +418,26 @@
     lax.fori_loop(first, 26 - first, plane, 0, unroll=4)
 
 
-def interpolate(ub, hb, ph, pw, zt, s, uh, ul, out):
+def interpolate(ub, hb, ph, pw, zt, s, scale, uh, ul, out):
     for x in range(20):
         row = jnp.concatenate([ub[0, x + 3, 0:40], ub[1, x + 3, 0:40], ub[2, x + 3, 0:40], hb[x + 3, 0:40]], axis=1)
         high, low = halves(row)
         uh[x * 40:(x + 1) * 40] = high
         ul[x * 40:(x + 1) * 40] = low
-    z, comp = edge_rows()
-    line = iota((128, 1), 0)
-    outside = ((z < 0) | (z >= CZ)) & (line < 64)
-
-    def chunk(pc, carry):
-        at = pl.ds(pl.multiple_of(pc * 256, 256), 256)
-        res = dot3((uh[...], ul[...]), (ph[:, at], pw[:, at]), TN)
+    field = uh[...].T[0:448], ul[...].T[0:448]
+    z, comp = (v[0:64] for v in edge_rows())
+    outside = (z < 0) | (z >= CZ)
+    for pc in range(4):
+        at = slice(pc * 256, (pc + 1) * 256)
+        res = dot3(field, (ph[:, at], pw[:, at]), NN)
         wz = zt[0:128, at]
-        rim = jnp.where(outside, zt[128:256, at] * res[384:512], 0.0)
-        alive = s[4, pc, 7:8, :]
+        rim = jnp.where(outside, zt[128:192, at] * res[384:448], 0.0)
+        factor = s[4, pc, 7:8, :] * scale[1, pc:pc + 1, :]
         for c in range(3):
-            value = jnp.sum(res[c * 128:(c + 1) * 128] * wz + jnp.where(comp == c, rim, 0.0), axis=0, keepdims=True)
-            out[c, pl.ds(2 * pc, 1), :] = (value * alive)[:, 0:128]
-            out[c, pl.ds(2 * pc + 1, 1), :] = (value * alive)[:, 128:256]
-        return carry
-
-    lax.fori_loop(0, 4, chunk, 0)
+            value = jnp.sum(res[c * 128:(c + 1) * 128] * wz, axis=0, keepdims=True)
+            value = (value + jnp.sum(jnp.where(comp == c, rim, 0.0), axis=0, keepdims=True)) * factor
+            out[c, 2 * pc:2 * pc + 1, :] = value[:, 0:128]
+            out[c, 2 * pc + 1:2 * pc + 2, :] = value[:, 128:256]
 
 
 def step_kernel(
@@ -417,7 +445,7 @@
     local_in, owner_in, partner_in, mask_in,
     field_out, vel_out,
     cell, offset, radius, force, visc, alive,
-    s, thick, zs, q, hot_p, hot_a, tab, mtab, mine, other, push, keys, acc, selves,
+    s, thick, scale, zs, q, hot_p, hot_a, tab, mine, other, push, keys, acc, selves,
     ry, rz, xs, rx1, rx2, loads,
     ph0, pw0, ph1, pw1, zt, pfy, pfd, zh, zl,
     bx, by, main, edge, pack, rim,
@@ -494,7 +522,12 @@
         for h in range(4):
             s[4, h, r:r + 1, 0:128] = v[2 * h:2 * h + 1]
             s[4, h, r:r + 1, 128:256] = v[2 * h + 1:2 * h + 2]
-    thick[4] = visc[...] * flags
+    for h in range(4):
+        scale[1, h:h + 1, :] = envelope_scale(s, 4, h)
+    for h in range(4):
+        for k in range(2):
+            row = slice(2 * h + k, 2 * h + k + 1)
+            thick[4, row, :] = visc[row, :] * flags[row] * scale[1, h:h + 1, k * 128:(k + 1) * 128]
     pl.semaphore_wait(barrier, len(greeted))
     start(s_x)
     start(s_z)
@@ -502,31 +535,34 @@
 
     bx[26:28] = jnp.zeros((2, CY, CZ), F32)
     hot_rows(q, hot_p, hot_a, 0)
-    find_mine(s.at[4], q, hot_a, mtab, mine, 0)
+    find_mine(s.at[4], q, mine, 0)
     arrived(s_z)
     arrived(q_z)
-    for l in (1, 2):
-        hot_rows(q, hot_p, hot_a, l)
-        find_mine(zs.at[l - 1], q, hot_a, mtab, mine, l)
+    hot_rows(q, hot_p, hot_a, 1)
+    find_mine(zs.at[0], q, mine, 1)
     arrived(s_x)
     start(s_y)
-    main[...] = jnp.zeros_like(main)
-    edge[...] = jnp.zeros_like(edge)
-    long_tables(s, 4, 0, 3, 20, ph0, pw0, zt.at[0])
+    hot_rows(q, hot_p, hot_a, 2)
+    find_mine(zs.at[1], q, mine, 2)
+    find_others(s, q, hot_p, tab, other, (3, 4, 5), True)
     arrived(s_y)
     start(b_x)
 
-    find_others(s, q, hot_p, tab, other)
+    find_others(s, q, hot_p, tab, other, (0, 1, 2, 6, 7, 8), False)
     push_forces(q, mine, other, push, keys)
-    sum_forces(push, keys, hot_p, hot_a, acc, selves)
-
+    sum_others(push, keys, hot_p, acc)
     start(a_y)
+    sum_mine(push, keys, hot_a, selves, 1)
+    sum_mine(push, keys, hot_a, selves, 2)
     start(a_z)
+    sum_mine(push, keys, hot_a, selves, 0)
+
+    long_tables(s, 4, 0, 3, 20, ph0, pw0, zt.at[0])
+
     def side_tables(it, carry):
         long_tables(s, 3 + 2 * it, 2 * it - 1, it * 19, 7, ph1.at[it], pw1.at[it], zt.at[1 + it])
         return carry
 
-    lax.fori_loop(0, 2, side_tables, 0)
     arrived(a_y)
     arrived(a_z)
     xs[...] = jnp.zeros_like(xs)
@@ -542,6 +578,26 @@
         xs[1, c * 4:c * 4 + 4] = middle[4:8] + f
         xs[2, c * 4:c * 4 + 4] = middle[8:12]
     start(a_x)
+
+    def thickness(b):
+        return jnp.concatenate([thick[b, t:t + 1, :] for t in range(8)], axis=1)
+
+    def forces(b):
+        return {c: line_of(loads, b, c) for c in range(3)}
+
+    def long_all(load, parts):
+        long_brick(ph0, pw0, zt.at[0], load(4), parts, main, edge, 3, 20)
+
+        def side(it, carry):
+            long_brick(ph1.at[it], pw1.at[it], zt.at[1 + it], load(3 + 2 * it), parts, main, edge, it * 19, 7)
+            return carry
+
+        lax.fori_loop(0, 2, side, 0)
+
+    lax.fori_loop(0, 2, side_tables, 0)
+    for h in range(4):
+        for n in (0, 2):
+            scale[n, h:h + 1, :] = envelope_scale(s, 3 + n, h)
     for n, dy in enumerate((-1, 1)):
         short_tables(s, 3 * (dy + 1) + 1, 0, dy, 3, 20, pfy.at[n], zh.at[n * 3], zl.at[n * 3])
 
@@ -551,35 +607,8 @@
             return carry
 
         lax.fori_loop(0, 2, corner, 0)
-
-    def thickness(b):
-        return {3: jnp.concatenate([thick[b, t:t + 1, :] for t in range(8)], axis=1)}
-
-    def short_all(load):
-        for n, dy in enumerate((-1, 1)):
-            k = n * 3
-            short_brick(pfy[n], zh.at[k], zl.at[k], load(3 * (dy + 1) + 1), main, edge, 3, 20, R0[dy + 1])
-
-            def corner(it, carry):
-                k = n * 3 + 1 + it
-                b = 3 * (dy + 1) + 2 * it
-                short_brick(pfd[n * 2 + it], zh.at[k], zl.at[k], load(b), main, edge, it * 19, 7, R0[dy + 1])
-                return carry
-
-            lax.fori_loop(0, 2, corner, 0)
-
-    def long_all(load, parts):
-        long_brick(ph0, pw0, zt.at[0], load(4), parts, main, edge, 3, 20)
-
-        def side(it, carry):
-            long_brick(ph1.at[it], pw1.at[it], zt.at[1 + it], load(3 + 2 * it), parts, main, edge, it * 19, 7)
-            return carry
-
-        lax.fori_loop(0, 2, side, 0)
-
-    long_all(thickness, (3, None))
-    short_all(thickness)
-
+    main[...] = jnp.zeros_like(main)
+    edge[...] = jnp.zeros_like(edge)
     arrived(a_x)
     for n in range(3):
         if n == 0:
@@ -589,7 +618,7 @@
         else:
             total = rx1[1, 1] + rx2[1] + xs[2]
         for h in range(4):
-            on = s[3 + n, h, 7:8, :]
+            on = s[3 + n, h, 7:8, :] * scale[n, h:h + 1, :]
             for c in range(3):
                 loads[3 + n, c * 4 + h:c * 4 + h + 1, :] = on * total[c * 4 + h:c * 4 + h + 1]
         loads[3 + n, 12:16] = jnp.zeros((4, 256), F32)
@@ -597,16 +626,27 @@
     arrived(b_x)
     start(b_y)
 
-    def forces(b):
-        return {c: line_of(loads, b, c) for c in range(3)}
-
+    long_all(lambda b: {3: thickness(b)}, (3, None))
     long_all(forces, (2, None))
     arrived(l_y)
-    short_all(forces)
+    for n, dy in enumerate((-1, 1)):
+        k = n * 3
+        b = 3 * (dy + 1) + 1
+        short_brick(pfy[n], zh.at[k], zl.at[k], {**forces(b), 3: thickness(b)}, main, edge, 3, 20, R0[dy + 1])
+
+        def corner(it, carry):
+            k = n * 3 + 1 + it
+            b = 3 * (dy + 1) + 2 * it
+            load = {**forces(b), 3: thickness(b)}
+            short_brick(pfd[n * 2 + it], zh.at[k], zl.at[k], load, main, edge, it * 19, 7, R0[dy + 1])
+            return carry
+
+        lax.fori_loop(0, 2, corner, 0, unroll=True)
     arrived(b_y)
-    wrap_rims(bx, by, main, edge, pack)
+    wrap_rims(bx, by, edge, pack)
     start(e_z)
     long_all(forces, (0, 1))
+    add_base(bx, by, main)
     arrived(e_z)
 
     first_sweep(main, edge, rim, ua, ha, inv, hvisco, hinv)
@@ -623,7 +663,7 @@
     lax.fori_loop(0, CX, finish, 0)
     outputs = [pltpu.make_async_copy(ua.at[:, pl.ds(0, CX), pl.ds(0, CY)], field_out, out_sem.at[0])]
     outputs[0].start()
-    interpolate(ub, hb, ph0, pw0, zt.at[0], s, uh, ul, vel)
+    interpolate(ub, hb, ph0, pw0, zt.at[0], s, scale, uh, ul, vel)
     outputs.append(pltpu.make_async_copy(vel, vel_out, out_sem.at[1]))
     outputs[1].start()
     for group in (s_x, s_y, s_z, q_z, b_x, b_y, a_y, a_z, a_x, l_y, e_z):
@@ -641,8 +681,8 @@
     sem = pltpu.SemaphoreType.DMA
     return [
         i(3, 8, 128), f(3, 8, 128), f(8, 128), f(3, 8, 128), f(8, 128), i(8, 128),
-        f(9, 4, 8, 256), f(9, 8, 128), f(2, 4, 8, 256), i(3, 4, 32, 128),
-        b(3, 256, PAIRS), b(3, 256, PAIRS), b(288, 512), b(32, 512),
+        f(9, 4, 8, 256), f(9, 8, 128), f(3, 8, 256), f(2, 4, 8, 256), i(3, 4, 32, 128),
+        b(3, 256, PAIRS), b(3, 256, PAIRS), b(192, 512),
         f(TILES, 8, 128), f(TILES, 8, 128), f(6, TILES, 128), i(2, TILES, 128),
         f(3, 40, 256), f(3, 24, 256),
         f(2, 3, 16, 256), f(2, 24, 256), f(3, 16, 256), f(2, 2, 16, 256), f(2, 16, 256), f(9, 16, 256),

time: 85.1 us -> 74.5 us (0.88)
  Pallas kernels: 80.4 us -> 69.7 us
    pallas_call x1, Pallas kernels: 80.4 us -> 69.7 us  [body(): pl.pallas_call(step_kernel, out_shape=(jax.ShapeDtypeStruct((3, CX, CY, C...]
where the time goes in v1:
time: 74.5 us; the launch traced here: 73 us
  Pallas kernels  69.7 us (94%)
  local copies, waits for them, and re-layouts  2.67 us (4%)
    pallas_call x1, Pallas kernels, body(): pl.pallas_call(step_kernel, out_shape=(jax.ShapeDtypeStruct((3, CX, CY, C...  69.7 us
    unnamed x4, local copies, waits for them, and re-layouts  2.67 us

profile of v1, /device:TPU:1, one launch (start us, length us, event | category | flops | bytes accessed | tf_op | source)
XLA Modules:
  0.0 73.0 jit_solution(13459771703176075522)
XLA Ops:
  0.6 69.7 %coupling.1 = (f32[3,16,32,128]{3,2,1,0:T(8,128)}, f32[3,8,128]{2,1,0:T(8,128)}) custom-call(s32[3,8,128]{2,1,0:T(8,128)} %bitcast.15, f32[3,8,128]{2,1,0:T(8,128)} %bitcast.16, f32[8,128]{1,0:T(8,128)} %bitcast.19, f32[3,8,128]{2,1,0:T(8,128)} %bitcast.17, f32[8,128]{1,0:T(8,128)} %bitcast.20, s32[8,128]{1,0:T(8,128)} %bitcast.21, f32[16,32,128]{2,1,0:T(8,128)} %base_in.1, ...), custom_call_target="tpu_custom_call" | custom-call | tf_op jit(solution)/shard_map/coupling/pallas_call | solution.py:706
  70.4 0.0 copy-start
  70.4 2.1 %copy.17 = f32[3,16,32,128]{3,2,1,0:T(8,128)} copy(f32[3,16,32,128]{3,2,1,0:T(8,128)} %get-tuple-element.12) | data formatting | bytes 1572864
  72.4 0.0 copy-done
  72.4 0.6 copy.18
Async XLA Ops:
  70.4 2.1 %copy-start = (f32[3,8,128]{2,1,0:T(8,128)S(1)}, f32[3,8,128]{2,1,0:T(8,128)}, u32[]{:S(2)}) copy-start(f32[3,8,128]{2,1,0:T(8,128)} %get-tuple-element.5) | copy-start | bytes 36868

commit v2 on v1

--- a/solution.py
+++ b/solution.py
@@ -112,7 +112,7 @@
             mine[l * (PAIRS // 128) + n] = out
         return carry
 
-    lax.fori_loop(0, PAIRS // 512, step, 0)
+    lax.fori_loop(0, PAIRS // 512, step, 0, unroll=4)
 
 
 def codes(own):
@@ -123,16 +123,14 @@
     return dx, dy, rest - 3 * dy
 
 
-def find_others(s, q, hot_p, tab, other, bricks, first):
+def find_others(s, q, hot_p, tab, tab_low, other, bricks, first):
     count = len(bricks)
-    def fill(brick, n):
-        v = jnp.concatenate([s[brick, 0], s[brick, 1], s[brick, 2], s[brick, 3]], axis=0)
-        high, low = halves(v)
-        tab[n * 32:(n + 1) * 32, 0:256] = high
-        tab[n * 32:(n + 1) * 32, 256:512] = low
-
     for n, brick in enumerate(bricks):
-        fill(brick, n)
+        v = jnp.concatenate([s[brick, h] for h in range(4)], axis=0)
+        high = v.astype(BF)
+        rest = v - high.astype(F32)
+        tab[n * 32:(n + 1) * 32] = high
+        tab_low[n * 16:(n + 1) * 16] = jnp.concatenate([rest[h * 8:h * 8 + 4] for h in range(4)], axis=0).astype(BF)
     slabs = [b * 4 + h for b in bricks for h in range(4)]
     tiles = QB // 128
 
@@ -142,18 +140,19 @@
         hot = hot_p[l, :, pl.ds(pl.multiple_of(ch * QB, QB), QB)]
         dx, dy, _ = codes(row_of(q, l, 1, ch))
         slab = (dy * 3 + dx) * 4 + (row_of(q, l, 2, ch) >> 8)
-        rows = slice(0, count * 32)
-        found = dot(tab[rows, 0:256], hot, NN) + dot(tab[rows, 256:512], hot, NN)
         if first:
             out = jnp.zeros((8, QB), F32)
         else:
             out = jnp.concatenate([other[it * tiles + t] for t in range(tiles)], axis=1)
-        out = pick(found, slab, slabs, out)
+        out = pick(dot(tab[0:count * 32], hot, NN), slab, slabs, out)
+        low = pick(dot(tab_low[0:count * 16], hot, NN), slab >> 1, [k // 2 for k in slabs[::2]], jnp.zeros((8, QB), F32))
+        low = jnp.where(slab & 1 == 1, low[4:8], low[0:4])
+        out = out + jnp.concatenate([low, jnp.zeros((4, QB), F32)], axis=0)
         for t in range(tiles):
             other[it * tiles + t] = out[:, t * 128:(t + 1) * 128]
         return carry
 
-    lax.fori_loop(0, 3 * PAIRS // QB, step, 0, unroll=2)
+    lax.fori_loop(0, 3 * PAIRS // QB, step, 0, unroll=4)
 
 
 def push_forces(q, mine, other, push, keys):
@@ -164,11 +163,11 @@
         m = [mine[at, r, :] for r in range(8)]
         o = [other[at, r, :] for r in range(8)]
         r = [
-            (o[c] - m[c]) + (o[3 + c] - m[3 + c]) + (code - 1).astype(F32) * float(side)
+            (o[4 + c] - m[4 + c]) + (o[c] - m[c]) + (code - 1).astype(F32) * float(side)
             for c, (code, side) in enumerate(((dx, CX), (dy, CY), (dz, CZ)))
         ]
         spacing = jnp.sqrt(r[0] * r[0] + r[1] * r[1] + r[2] * r[2])
-        clearance = spacing - m[6] - o[6]
+        clearance = spacing - m[3] - o[3]
         want = (1, 2, 0)[l]
         weight = (
             jnp.where(dz == want, live, 0).astype(F32) * m[7] * o[7] * lubrication_strength
@@ -203,7 +202,7 @@
         acc[...] -= (sums[0:120] + sums[120:240]).reshape(3, 40, 256)
         return carry
 
-    lax.fori_loop(0, 3 * PAIRS // QB, step, 0, unroll=2)
+    lax.fori_loop(0, 3 * PAIRS // QB, step, 0, unroll=4)
 
 
 def sum_mine(push, keys, hot_a, selves, l):
@@ -234,13 +233,14 @@
 
 def axis_tables(s, b, kc, dx, dy, x0, nx, r0, ny):
     v = s[b, kc]
-    offs = [v[3 + c:4 + c] for c in range(3)]
+    offs = [v[c:c + 1] for c in range(3)]
+    cells = [v[4 + c:5 + c] for c in range(3)]
     dx_cells = jnp.asarray(dx * CX, jnp.int32).astype(F32)
-    wx = window(v[0:1] + dx_cells, iota((nx, 256), 0) + (x0 - REACH), offs[0])
-    wy = window(v[1:2] + float(dy * CY), iota((ny, 256), 0) + (r0 - ROW0), offs[1])
-    wz = window(v[2:3], iota((128, 256), 0), offs[2])
+    wx = window(cells[0] + dx_cells, iota((nx, 256), 0) + (x0 - REACH), offs[0])
+    wy = window(cells[1] + float(dy * CY), iota((ny, 256), 0) + (r0 - ROW0), offs[1])
+    wz = window(cells[2], iota((128, 256), 0), offs[2])
     eight = iota((8, 256), 0)
-    wedge = [window(v[2:3], eight + z, offs[2]) for z in (-5, 125, -3, 123)]
+    wedge = [window(cells[2], eight + z, offs[2]) for z in (-5, 125, -3, 123)]
     return wx, wy, wz, [w for w in wedge for c in range(4)]
 
 
@@ -281,31 +281,29 @@
 
 def envelope_scale(s, b, h):
     total = norm(s[b, h])
-    return 1.0 / (total[3:4] * total[4:5] * total[5:6])
+    return 1.0 / (total[0:1] * total[1:2] * total[2:3])
 
 
 def line_of(ref, b, c):
     return jnp.concatenate([ref[b, c * 4 + h:c * 4 + h + 1, :] for h in range(4)], axis=1)
 
 
-def long_brick(ph, pw, zt, load, parts, main, edge, x0, nx):
+def long_brick(ph, pw, zt, load, main, x0, nx):
+    d = halves(jnp.concatenate([zt[0:128, :] * v for v in load.values()], axis=0))
+    res = dot3((ph[...], pw[...]), d, NT).reshape(nx, 40, 256)
+    for n, c in enumerate(load):
+        main[c, pl.ds(x0, nx), 0:40, :] += res[:, :, n * 128:(n + 1) * 128]
+
+
+def long_edge(ph, pw, zt, load, edge, x0, nx):
     comp = edge_rows()[1]
-    cols = []
-    for part in parts:
-        if part is None:
-            v = jnp.zeros((128, SLOTS), F32)
-            for c, value in load.items():
-                v = jnp.where(comp == c, value, v)
-            cols.append(zt[128:256, :] * v)
-        else:
-            cols.append(zt[0:128, :] * load[part])
-    res = dot3((ph[...], pw[...]), halves(jnp.concatenate(cols, axis=0)), NT).reshape(nx, 40, 256)
-    for n, part in enumerate(parts):
-        here = res[:, :, n * 128:(n + 1) * 128]
-        if part is None:
-            edge[pl.ds(x0, nx), 0:40, :] += here
-        else:
-            main[part, pl.ds(x0, nx), 0:40, :] += here
+    v = jnp.zeros((128, SLOTS), F32)
+    for c, value in load.items():
+        v = jnp.where(comp == c, value, v)
+    high, low = halves(zt[128:256, :] * v)
+    res = dot(ph[...], jnp.concatenate([high, low], axis=0), NT)
+    res = res[:, 0:128] + res[:, 128:256] + dot(pw[...], high, NT)
+    edge[pl.ds(x0, nx), 0:40, :] += res.reshape(nx, 40, 128)
 
 
 def short_brick(pf, zh, zl, load, main, edge, x0, nx, r0):
@@ -362,16 +360,20 @@
     lax.fori_loop(0, PLANES // 4, plane, 0)
 
 
-def first_sweep(main, edge, rim, ua, ha, inv, hvisco, hinv):
+def first_sweep(main, edge, rim, ua, ha, inv, hvisco, hinv, got_high, got_low):
     lane = iota((ROWS, 128), 1)
     thick = lane // 32 * 32 + 24 + lane % 8
 
-    def start(g, carry):
+    def unpack(g, carry):
         from_low, from_high = rim[0, g], rim[1, g]
         for j in range(4):
             i = g * 4 + j
             got = jnp.where(lane < 32, roll(from_low, -32 * j, 1), 0.0)
             got = jnp.where(lane // 32 == 1, roll(from_high, 32 - 32 * j, 1), got)
+            high, low = halves(got)
+            at = pl.ds(pl.multiple_of(i * ROWS, ROWS), ROWS)
+            got_high[at] = high
+            got_low[at] = low
             total = jnp.where(lane < 64, edge[i], 0.0) + got
             v = lanes(total, thick)
             r = 1.0 / (damping + 6.0 * v)
@@ -379,19 +381,28 @@
             hinv[i] = r
             edge[i] = total
             ha[i] = total * r
-            m = []
-            for c in range(4):
-                near = lanes(got, jnp.where(lane < 64, lane + (c * 8 + 5), lane + (33 + c * 8 - 126)) % 128)
-                m.append(main[c, i] + jnp.where((lane < 2) | (lane >= 126), near, 0.0))
-            main[3, i] = m[3]
-            r = 1.0 / (damping + 6.0 * m[3])
-            inv[i] = r
-            for c in range(3):
-                main[c, i] = m[c]
-                ua[c, i] = m[c] * r
-        return carry
-
-    lax.fori_loop(0, PLANES // 4, start, 0)
+        return carry
+
+    lax.fori_loop(0, PLANES // 4, unpack, 0)
+
+    source, col = iota((128, 256), 0), iota((128, 256), 1)
+    z = col & 127
+    for c in (0, 2):
+        wanted = jnp.where(z < 2, z + 5, z + (33 - 126)) + (c + (col >> 7)) * 8
+        ones = jnp.where((source == wanted) & ((z < 2) | (z >= 126)), 1.0, 0.0).astype(BF)
+        near = dot(got_high[...], ones, NN) + dot(got_low[...], ones, NN)
+        near = near.reshape(PLANES, ROWS, 256)
+        main[c] += near[:, :, 0:128]
+        main[c + 1] += near[:, :, 128:256]
+
+    def start(i, carry):
+        r = 1.0 / (damping + 6.0 * main[3, i])
+        inv[i] = r
+        for c in range(3):
+            ua[c, i] = main[c, i] * r
+        return carry
+
+    lax.fori_loop(0, PLANES, start, 0, unroll=4)
 
 
 def sweep(src, dst, hsrc, hdst, main, edge, inv, hvisco, hinv, first, rows):
@@ -415,7 +426,7 @@
             dst[c, i, at] = (main[c, i, at] + v * beside) * r
         return carry
 
-    lax.fori_loop(first, 26 - first, plane, 0, unroll=4)
+    lax.fori_loop(first, 26 - first, plane, 0, unroll=True)
 
 
 def interpolate(ub, hb, ph, pw, zt, s, scale, uh, ul, out):
@@ -445,11 +456,11 @@
     local_in, owner_in, partner_in, mask_in,
     field_out, vel_out,
     cell, offset, radius, force, visc, alive,
-    s, thick, scale, zs, q, hot_p, hot_a, tab, mine, other, push, keys, acc, selves,
+    s, thick, scale, zs, q, hot_p, hot_a, tab, tab_low, mine, other, push, keys, acc, selves,
     ry, rz, xs, rx1, rx2, loads,
     ph0, pw0, ph1, pw1, zt, pfy, pfd, zh, zl,
     bx, by, main, edge, pack, rim,
-    ua, ub, ha, hb, inv, hvisco, hinv, uh, ul, vel,
+    ua, ub, ha, hb, inv, hvisco, hinv, got_high, got_low, uh, ul, vel,
     in_sem, send_sem, recv_sem, out_sem,
 ):
     me = {a: lax.axis_index(a) for a in ("gx", "gy", "gz")}
@@ -517,7 +528,7 @@
     for c in inputs:
         c.wait()
     flags = alive[...].astype(F32)
-    rows = [cell[c].astype(F32) for c in range(3)] + [offset[c] for c in range(3)] + [radius[...], flags]
+    rows = [offset[c] for c in range(3)] + [radius[...]] + [cell[c].astype(F32) for c in range(3)] + [flags]
     for r, v in enumerate(rows):
         for h in range(4):
             s[4, h, r:r + 1, 0:128] = v[2 * h:2 * h + 1]
@@ -540,15 +551,15 @@
     arrived(q_z)
     hot_rows(q, hot_p, hot_a, 1)
     find_mine(zs.at[0], q, mine, 1)
+    hot_rows(q, hot_p, hot_a, 2)
+    find_mine(zs.at[1], q, mine, 2)
     arrived(s_x)
     start(s_y)
-    hot_rows(q, hot_p, hot_a, 2)
-    find_mine(zs.at[1], q, mine, 2)
-    find_others(s, q, hot_p, tab, other, (3, 4, 5), True)
+    find_others(s, q, hot_p, tab, tab_low, other, (3, 4, 5), True)
     arrived(s_y)
     start(b_x)
 
-    find_others(s, q, hot_p, tab, other, (0, 1, 2, 6, 7, 8), False)
+    find_others(s, q, hot_p, tab, tab_low, other, (0, 1, 2, 6, 7, 8), False)
     push_forces(q, mine, other, push, keys)
     sum_others(push, keys, hot_p, acc)
     start(a_y)
@@ -585,14 +596,21 @@
     def forces(b):
         return {c: line_of(loads, b, c) for c in range(3)}
 
-    def long_all(load, parts):
-        long_brick(ph0, pw0, zt.at[0], load(4), parts, main, edge, 3, 20)
+    def everything(b):
+        return {**forces(b), 3: thickness(b)}
+
+    def long_all(comps, what, *out):
+        def part(b):
+            load = everything(b)
+            return {c: load[c] for c in comps}
+
+        what(ph0, pw0, zt.at[0], part(4), *out, 3, 20)
 
         def side(it, carry):
-            long_brick(ph1.at[it], pw1.at[it], zt.at[1 + it], load(3 + 2 * it), parts, main, edge, it * 19, 7)
+            what(ph1.at[it], pw1.at[it], zt.at[1 + it], part(3 + 2 * it), *out, it * 19, 7)
             return carry
 
-        lax.fori_loop(0, 2, side, 0)
+        lax.fori_loop(0, 2, side, 0, unroll=True)
 
     lax.fori_loop(0, 2, side_tables, 0)
     for h in range(4):
@@ -626,18 +644,17 @@
     arrived(b_x)
     start(b_y)
 
-    long_all(lambda b: {3: thickness(b)}, (3, None))
-    long_all(forces, (2, None))
+    long_all(range(4), long_edge, edge)
     arrived(l_y)
     for n, dy in enumerate((-1, 1)):
         k = n * 3
         b = 3 * (dy + 1) + 1
-        short_brick(pfy[n], zh.at[k], zl.at[k], {**forces(b), 3: thickness(b)}, main, edge, 3, 20, R0[dy + 1])
+        short_brick(pfy[n], zh.at[k], zl.at[k], everything(b), main, edge, 3, 20, R0[dy + 1])
 
         def corner(it, carry):
             k = n * 3 + 1 + it
             b = 3 * (dy + 1) + 2 * it
-            load = {**forces(b), 3: thickness(b)}
+            load = everything(b)
             short_brick(pfd[n * 2 + it], zh.at[k], zl.at[k], load, main, edge, it * 19, 7, R0[dy + 1])
             return carry
 
@@ -645,11 +662,12 @@
     arrived(b_y)
     wrap_rims(bx, by, edge, pack)
     start(e_z)
-    long_all(forces, (0, 1))
+    long_all((0, 1), long_brick, main)
+    long_all((2, 3), long_brick, main)
     add_base(bx, by, main)
     arrived(e_z)
 
-    first_sweep(main, edge, rim, ua, ha, inv, hvisco, hinv)
+    first_sweep(main, edge, rim, ua, ha, inv, hvisco, hinv, got_high, got_low)
     rest = (main, edge, inv, hvisco, hinv)
     sweep(ua, ub, ha, hb, *rest, 1, 48)
     sweep(ub, ua, hb, ha, *rest, 2, 40)
@@ -673,6 +691,17 @@
         c.wait()
 
 
+def hand_over(field, velocity, field_out, velocity_out, sem):
+    copies = [pltpu.make_async_copy(velocity, velocity_out, sem.at[12])]
+    for n in range(12):
+        at = (n // 4, pl.ds(n % 4 * 4, 4))
+        copies.append(pltpu.make_async_copy(field.at[at], field_out.at[at], sem.at[n]))
+    for c in copies:
+        c.start()
+    for c in copies:
+        c.wait()
+
+
 def scratch():
     f = lambda *shape: pltpu.VMEM(shape, F32)
     i = lambda *shape: pltpu.VMEM(shape, jnp.int32)
@@ -682,14 +711,14 @@
     return [
         i(3, 8, 128), f(3, 8, 128), f(8, 128), f(3, 8, 128), f(8, 128), i(8, 128),
         f(9, 4, 8, 256), f(9, 8, 128), f(3, 8, 256), f(2, 4, 8, 256), i(3, 4, 32, 128),
-        b(3, 256, PAIRS), b(3, 256, PAIRS), b(192, 512),
+        b(3, 256, PAIRS), b(3, 256, PAIRS), b(192, 256), b(96, 256),
         f(TILES, 8, 128), f(TILES, 8, 128), f(6, TILES, 128), i(2, TILES, 128),
         f(3, 40, 256), f(3, 24, 256),
         f(2, 3, 16, 256), f(2, 24, 256), f(3, 16, 256), f(2, 2, 16, 256), f(2, 16, 256), f(9, 16, 256),
         b(800, SLOTS), b(800, SLOTS), b(2, 280, SLOTS), b(2, 280, SLOTS), f(3, 256, SLOTS),
         f(2, 160, SLOTS), f(4, 56, SLOTS), b(6, 256, SLOTS), b(6, 256, SLOTS),
         f(PLANES, CY, CZ), f(2, PLANES, 8, CZ), grid(4), grid(), f(2, PLANES // 4, ROWS, 128), f(2, PLANES // 4, ROWS, 128),
-        grid(3), grid(3), grid(), grid(), grid(), grid(), grid(), b(800, 512), b(800, 512), f(3, 8, 128),
+        grid(3), grid(3), grid(), grid(), grid(), grid(), grid(), b(PLANES * ROWS, 128), b(PLANES * ROWS, 128), b(800, 512), b(800, 512), f(3, 8, 128),
         sem((11,)), sem((28,)), sem((28,)), sem((2,)),
     ]
 
@@ -703,20 +732,34 @@
     )]
     args += [base_viscosity]
     args += [a.reshape(32, 128) for a in (pair_local, pair_owner, pair_partner, pair_slot_mask)]
-    field, velocity = pl.pallas_call(
+    hbm = pl.BlockSpec(memory_space=pltpu.HBM)
+    results = (
+        jax.ShapeDtypeStruct((3, CX, CY, CZ), F32),
+        jax.ShapeDtypeStruct((3, 8, 128), F32),
+    )
+    results = pl.pallas_call(
         step_kernel,
-        out_shape=(
-            jax.ShapeDtypeStruct((3, CX, CY, CZ), F32),
-            jax.ShapeDtypeStruct((3, 8, 128), F32),
-        ),
-        in_specs=[pl.BlockSpec(memory_space=pltpu.HBM)] * 11,
-        out_specs=(pl.BlockSpec(memory_space=pltpu.HBM),) * 2,
+        out_shape=results,
+        in_specs=[hbm] * 11,
+        out_specs=(hbm,) * 2,
         scratch_shapes=scratch(),
         compiler_params=pltpu.CompilerParams(
             collective_id=0, has_side_effects=True, vmem_limit_bytes=62 * 2**20
         ),
         name="coupling",
     )(*args)
+    field, velocity = pl.pallas_call(
+        hand_over,
+        out_shape=(
+            jax.ShapeDtypeStruct((3, CX, CY, CZ), F32),
+            jax.ShapeDtypeStruct((3, 8, 128), F32),
+        ),
+        in_specs=[hbm] * 2,
+        out_specs=(hbm,) * 2,
+        scratch_shapes=[pltpu.SemaphoreType.DMA((13,))],
+        compiler_params=pltpu.CompilerParams(vmem_limit_bytes=62 * 2**20),
+        name="hand_over",
+    )(*results)
     return field, velocity.reshape(3, 1, 1, 1, SLOTS)
 
 

time: 74.5 us -> 93 us (1.25); the launches traced: 73 us -> 92.9 us
  Pallas kernels: 69.7 us -> 92.1 us
  local copies, waits for them, and re-layouts: 2.67 us -> 0 us
    pallas_call x1 -> x2, Pallas kernels: 69.7 us -> 92.1 us  [the longest x1 66.6 us: body(): pl.pallas_call(step_kernel, out_shape=results, in_specs=[hbm] * 11, out_s...]
    unnamed x4 -> x0, local copies, waits for them, and re-layouts: 2.67 us -> none
where the time goes in v2:
time: 93 us; the launch traced here: 92.9 us
  Pallas kernels  92.1 us (99%)
    pallas_call x1, Pallas kernels, body(): pl.pallas_call(step_kernel, out_shape=results, in_specs=[hbm] * 11, out_s...  66.6 us
    pallas_call x1, Pallas kernels, body(): pl.pallas_call(hand_over, out_shape=(jax.ShapeDtypeStruct((3, CX, CY, CZ)...  25.4 us

profile of v2, /device:TPU:1, one launch (start us, length us, event | category | flops | bytes accessed | tf_op | source)
XLA Modules:
  0.0 92.9 jit_solution(6019001333112954276)
XLA Ops:
  0.6 66.6 %coupling.1 = (f32[3,16,32,128]{3,2,1,0:T(8,128)}, f32[3,8,128]{2,1,0:T(8,128)}) custom-call(s32[3,8,128]{2,1,0:T(8,128)} %bitcast.15, f32[3,8,128]{2,1,0:T(8,128)} %bitcast.16, f32[8,128]{1,0:T(8,128)} %bitcast.18, f32[3,8,128]{2,1,0:T(8,128)} %bitcast.17, f32[8,128]{1,0:T(8,128)} %bitcast.19, s32[8,128]{1,0:T(8,128)} %bitcast.20, f32[16,32,128]{2,1,0:T(8,128)} %base_in.1, ...), custom_call_target="tpu_custom_call" | custom-call | tf_op jit(solution)/shard_map/coupling/pallas_call | solution.py:740
  67.3 25.4 %hand_over.1 = (f32[3,16,32,128]{3,2,1,0:T(8,128)}, f32[3,8,128]{2,1,0:T(8,128)}) custom-call(f32[3,16,32,128]{3,2,1,0:T(8,128)} %get-tuple-element.6.field, f32[3,8,128]{2,1,0:T(8,128)} %get-tuple-element.7.velocity), custom_call_target="tpu_custom_call" | custom-call | tf_op jit(solution)/shard_map/hand_over/pallas_call | solution.py:751

commit v3 on v2

--- a/solution.py
+++ b/solution.py
@@ -295,15 +295,24 @@
         main[c, pl.ds(x0, nx), 0:40, :] += res[:, :, n * 128:(n + 1) * 128]
 
 
+def narrow(ph, pw, d, nx):
+    high, low = halves(d)
+    res = dot(ph[...], jnp.concatenate([high, low], axis=0), NT)
+    res = res[:, 0:128] + res[:, 128:256] + dot(pw[...], high, NT)
+    return res.reshape(nx, 40, 128)
+
+
+def long_one(ph, pw, zt, load, main, x0, nx):
+    (c, v), = load.items()
+    main[c, pl.ds(x0, nx), 0:40, :] += narrow(ph, pw, zt[0:128, :] * v, nx)
+
+
 def long_edge(ph, pw, zt, load, edge, x0, nx):
     comp = edge_rows()[1]
     v = jnp.zeros((128, SLOTS), F32)
     for c, value in load.items():
         v = jnp.where(comp == c, value, v)
-    high, low = halves(zt[128:256, :] * v)
-    res = dot(ph[...], jnp.concatenate([high, low], axis=0), NT)
-    res = res[:, 0:128] + res[:, 128:256] + dot(pw[...], high, NT)
-    edge[pl.ds(x0, nx), 0:40, :] += res.reshape(nx, 40, 128)
+    edge[pl.ds(x0, nx), 0:40, :] += narrow(ph, pw, zt[128:256, :] * v, nx)
 
 
 def short_brick(pf, zh, zl, load, main, edge, x0, nx, r0):
@@ -555,9 +564,12 @@
     find_mine(zs.at[1], q, mine, 2)
     arrived(s_x)
     start(s_y)
+    start(b_x)
     find_others(s, q, hot_p, tab, tab_low, other, (3, 4, 5), True)
+    long_tables(s, 4, 0, 3, 20, ph0, pw0, zt.at[0])
+    main[...] = jnp.zeros_like(main)
+    edge[...] = jnp.zeros_like(edge)
     arrived(s_y)
-    start(b_x)
 
     find_others(s, q, hot_p, tab, tab_low, other, (0, 1, 2, 6, 7, 8), False)
     push_forces(q, mine, other, push, keys)
@@ -568,12 +580,11 @@
     start(a_z)
     sum_mine(push, keys, hot_a, selves, 0)
 
-    long_tables(s, 4, 0, 3, 20, ph0, pw0, zt.at[0])
-
     def side_tables(it, carry):
         long_tables(s, 3 + 2 * it, 2 * it - 1, it * 19, 7, ph1.at[it], pw1.at[it], zt.at[1 + it])
         return carry
 
+    lax.fori_loop(0, 2, side_tables, 0)
     arrived(a_y)
     arrived(a_z)
     xs[...] = jnp.zeros_like(xs)
@@ -601,8 +612,7 @@
 
     def long_all(comps, what, *out):
         def part(b):
-            load = everything(b)
-            return {c: load[c] for c in comps}
+            return {c: thickness(b) if c == 3 else line_of(loads, b, c) for c in comps}
 
         what(ph0, pw0, zt.at[0], part(4), *out, 3, 20)
 
@@ -612,7 +622,6 @@
 
         lax.fori_loop(0, 2, side, 0, unroll=True)
 
-    lax.fori_loop(0, 2, side_tables, 0)
     for h in range(4):
         for n in (0, 2):
             scale[n, h:h + 1, :] = envelope_scale(s, 3 + n, h)
@@ -625,8 +634,7 @@
             return carry
 
         lax.fori_loop(0, 2, corner, 0)
-    main[...] = jnp.zeros_like(main)
-    edge[...] = jnp.zeros_like(edge)
+    long_all((3,), long_one, main)
     arrived(a_x)
     for n in range(3):
         if n == 0:
@@ -663,7 +671,7 @@
     wrap_rims(bx, by, edge, pack)
     start(e_z)
     long_all((0, 1), long_brick, main)
-    long_all((2, 3), long_brick, main)
+    long_all((2,), long_one, main)
     add_base(bx, by, main)
     arrived(e_z)
 
@@ -691,14 +699,17 @@
         c.wait()
 
 
-def hand_over(field, velocity, field_out, velocity_out, sem):
-    copies = [pltpu.make_async_copy(velocity, velocity_out, sem.at[12])]
-    for n in range(12):
-        at = (n // 4, pl.ds(n % 4 * 4, 4))
-        copies.append(pltpu.make_async_copy(field.at[at], field_out.at[at], sem.at[n]))
-    for c in copies:
+def hand_over(field, velocity, field_out, velocity_out, here, there, sem):
+    halves_of = [(c, pl.ds(n * 8, 8)) for c in range(3) for n in range(2)]
+    ways = [(velocity, there, velocity_out)] + [(field.at[at], here.at[at], field_out.at[at]) for at in halves_of]
+    arrive = [pltpu.make_async_copy(a, b, sem.at[0, n]) for n, (a, b, _) in enumerate(ways)]
+    leave = [pltpu.make_async_copy(b, c, sem.at[1, n]) for n, (_, b, c) in enumerate(ways)]
+    for c in arrive:
         c.start()
-    for c in copies:
+    for a, b in zip(arrive, leave):
+        a.wait()
+        b.start()
+    for c in leave:
         c.wait()
 
 
@@ -756,7 +767,9 @@
         ),
         in_specs=[hbm] * 2,
         out_specs=(hbm,) * 2,
-        scratch_shapes=[pltpu.SemaphoreType.DMA((13,))],
+        scratch_shapes=[
+            pltpu.VMEM((3, CX, CY, CZ), F32), pltpu.VMEM((3, 8, 128), F32), pltpu.SemaphoreType.DMA((2, 7)),
+        ],
         compiler_params=pltpu.CompilerParams(vmem_limit_bytes=62 * 2**20),
         name="hand_over",
     )(*results)

time: 93 us -> 71.6 us (0.77)
  Pallas kernels: 92.1 us -> 70.5 us
    pallas_call x1, Pallas kernels: 25.4 us -> 2 us  [body(): pl.pallas_call(hand_over, out_shape=(jax.ShapeDtypeStruct((3, CX, CY, CZ)...]
    pallas_call x1, Pallas kernels: 66.6 us -> 68.5 us  [body(): pl.pallas_call(step_kernel, out_shape=results, in_specs=[hbm] * 11, out_s...]
where the time goes in v3:
time: 71.6 us; the launch traced here: 71.3 us
  Pallas kernels  70.5 us (98%)
  between operations  0.82 us (1%)
    pallas_call x1, Pallas kernels, body(): pl.pallas_call(step_kernel, out_shape=results, in_specs=[hbm] * 11, out_s...  68.5 us
    pallas_call x1, Pallas kernels, body(): pl.pallas_call(hand_over, out_shape=(jax.ShapeDtypeStruct((3, CX, CY, CZ)...  2 us

profile of v3, /device:TPU:1, one launch (start us, length us, event | category | flops | bytes accessed | tf_op | source)
XLA Modules:
  0.0 71.3 jit_solution(3287341113717097013)
XLA Ops:
  0.6 68.5 %coupling.1 = (f32[3,16,32,128]{3,2,1,0:T(8,128)}, f32[3,8,128]{2,1,0:T(8,128)}) custom-call(s32[3,8,128]{2,1,0:T(8,128)} %bitcast.15, f32[3,8,128]{2,1,0:T(8,128)} %bitcast.16, f32[8,128]{1,0:T(8,128)} %bitcast.18, f32[3,8,128]{2,1,0:T(8,128)} %bitcast.17, f32[8,128]{1,0:T(8,128)} %bitcast.19, s32[8,128]{1,0:T(8,128)} %bitcast.20, f32[16,32,128]{2,1,0:T(8,128)} %base_in.1, ...), custom_call_target="tpu_custom_call" | custom-call | tf_op jit(solution)/shard_map/coupling/pallas_call | solution.py:751
  69.1 2.0 %hand_over.1 = (f32[3,16,32,128]{3,2,1,0:T(8,128)}, f32[3,8,128]{2,1,0:T(8,128)}) custom-call(f32[3,16,32,128]{3,2,1,0:T(8,128)} %get-tuple-element.6.field, f32[3,8,128]{2,1,0:T(8,128)} %get-tuple-element.7.velocity), custom_call_target="tpu_custom_call" | custom-call | tf_op jit(solution)/shard_map/hand_over/pallas_call | solution.py:762

commit v4 on v3

--- a/solution.py
+++ b/solution.py
@@ -513,10 +513,14 @@
         copy(bx.at[pl.ds(CX, REACH)], bx.at[pl.ds(0, REACH)], "gx", 1),
         copy(bx.at[pl.ds(REACH, REACH)], bx.at[pl.ds(CX + REACH, REACH)], "gx", -1),
     ]
-    b_y = [
-        copy(bx.at[:, pl.ds(CY - 8, 8)], by.at[0], "gy", 1),
-        copy(bx.at[:, pl.ds(0, 8)], by.at[1], "gy", -1),
-    ]
+    def base_rows(planes):
+        return [
+            copy(bx.at[planes, pl.ds(CY - 8, 8)], by.at[0, planes], "gy", 1),
+            copy(bx.at[planes, pl.ds(0, 8)], by.at[1, planes], "gy", -1),
+        ]
+
+    b_own = base_rows(pl.ds(REACH, CX))
+    b_far = base_rows(pl.ds(0, REACH)) + base_rows(pl.ds(REACH + CX, PLANES - REACH - CX))
     a_y = [copy(acc.at[:, pl.ds(24, 16)], ry.at[0], "gy", 1), copy(acc.at[:, pl.ds(0, 16)], ry.at[1], "gy", -1)]
     a_z = [copy(selves.at[1], rz.at[0], "gz", -1), copy(selves.at[2], rz.at[1], "gz", 1)]
     a_x = [
@@ -552,6 +556,7 @@
     start(s_x)
     start(s_z)
     start(q_z)
+    start(b_own)
 
     bx[26:28] = jnp.zeros((2, CY, CZ), F32)
     hot_rows(q, hot_p, hot_a, 0)
@@ -564,12 +569,12 @@
     find_mine(zs.at[1], q, mine, 2)
     arrived(s_x)
     start(s_y)
-    start(b_x)
     find_others(s, q, hot_p, tab, tab_low, other, (3, 4, 5), True)
     long_tables(s, 4, 0, 3, 20, ph0, pw0, zt.at[0])
     main[...] = jnp.zeros_like(main)
     edge[...] = jnp.zeros_like(edge)
     arrived(s_y)
+    start(b_x)
 
     find_others(s, q, hot_p, tab, tab_low, other, (0, 1, 2, 6, 7, 8), False)
     push_forces(q, mine, other, push, keys)
@@ -650,7 +655,7 @@
         loads[3 + n, 12:16] = jnp.zeros((4, 256), F32)
     start(l_y)
     arrived(b_x)
-    start(b_y)
+    start(b_far)
 
     long_all(range(4), long_edge, edge)
     arrived(l_y)
@@ -667,7 +672,8 @@
             return carry
 
         lax.fori_loop(0, 2, corner, 0, unroll=True)
-    arrived(b_y)
+    arrived(b_own)
+    arrived(b_far)
     wrap_rims(bx, by, edge, pack)
     start(e_z)
     long_all((0, 1), long_brick, main)
@@ -692,7 +698,7 @@
     interpolate(ub, hb, ph0, pw0, zt.at[0], s, scale, uh, ul, vel)
     outputs.append(pltpu.make_async_copy(vel, vel_out, out_sem.at[1]))
     outputs[1].start()
-    for group in (s_x, s_y, s_z, q_z, b_x, b_y, a_y, a_z, a_x, l_y, e_z):
+    for group in (s_x, s_y, s_z, q_z, b_x, b_own, b_far, a_y, a_z, a_x, l_y, e_z):
         for c in group:
             c.wait_send()
     for c in outputs:
@@ -730,7 +736,7 @@
         f(2, 160, SLOTS), f(4, 56, SLOTS), b(6, 256, SLOTS), b(6, 256, SLOTS),
         f(PLANES, CY, CZ), f(2, PLANES, 8, CZ), grid(4), grid(), f(2, PLANES // 4, ROWS, 128), f(2, PLANES // 4, ROWS, 128),
         grid(3), grid(3), grid(), grid(), grid(), grid(), grid(), b(PLANES * ROWS, 128), b(PLANES * ROWS, 128), b(800, 512), b(800, 512), f(3, 8, 128),
-        sem((11,)), sem((28,)), sem((28,)), sem((2,)),
+        sem((11,)), sem((32,)), sem((32,)), sem((2,)),
     ]
 
 

time: 71.6 us -> 70.9 us (level)
  no operation moved by 1% of the time
where the time goes in v4:
time: 70.9 us; the launch traced here: 70.6 us
  Pallas kernels  69.8 us (98%)
  between operations  0.82 us (1%)
    pallas_call x1, Pallas kernels, body(): pl.pallas_call(step_kernel, out_shape=results, in_specs=[hbm] * 11, out_s...  67.8 us
    pallas_call x1, Pallas kernels, body(): pl.pallas_call(hand_over, out_shape=(jax.ShapeDtypeStruct((3, CX, CY, CZ)...  2 us

profile of v4, /device:TPU:1, one launch (start us, length us, event | category | flops | bytes accessed | tf_op | source)
XLA Modules:
  0.0 70.6 jit_solution(11670694257689094086)
XLA Ops:
  0.6 67.8 %coupling.1 = (f32[3,16,32,128]{3,2,1,0:T(8,128)}, f32[3,8,128]{2,1,0:T(8,128)}) custom-call(s32[3,8,128]{2,1,0:T(8,128)} %bitcast.15, f32[3,8,128]{2,1,0:T(8,128)} %bitcast.16, f32[8,128]{1,0:T(8,128)} %bitcast.18, f32[3,8,128]{2,1,0:T(8,128)} %bitcast.17, f32[8,128]{1,0:T(8,128)} %bitcast.19, s32[8,128]{1,0:T(8,128)} %bitcast.20, f32[16,32,128]{2,1,0:T(8,128)} %base_in.1, ...), custom_call_target="tpu_custom_call" | custom-call | tf_op jit(solution)/shard_map/coupling/pallas_call | solution.py:757
  68.4 2.0 %hand_over.1 = (f32[3,16,32,128]{3,2,1,0:T(8,128)}, f32[3,8,128]{2,1,0:T(8,128)}) custom-call(f32[3,16,32,128]{3,2,1,0:T(8,128)} %get-tuple-element.6.field, f32[3,8,128]{2,1,0:T(8,128)} %get-tuple-element.7.velocity), custom_call_target="tpu_custom_call" | custom-call | tf_op jit(solution)/shard_map/hand_over/pallas_call | solution.py:768
